TPU v7x, 128 devices: a whole 4x4x4 slice. The times are simulated.
128 devices in a mesh: fr: 8 (over x, core), fc: 8 (over z_lo, y), cam: 2 (over z_hi).
Axes of the slice: x: 4, y: 4, z: 4 (z_hi: 2, z_lo: 2; z = z_hi * 2 + z_lo), core: 2. Of those that a mesh axis runs over, the one named last changes fastest.
Arguments:
- view_a: bfloat16 [4096, 8192], P(('fc', 'cam'), 'fr'), may hold values from -64 to 64
- view_b: bfloat16 [4096, 8192], P(('fr', 'cam'), 'fc'), may hold values from -64 to 64
Outputs:
- grad_a: bfloat16 [4096, 8192], P(('fc', 'cam'), 'fr')
- grad_b: bfloat16 [4096, 8192], P(('fr', 'cam'), 'fc')
- loss: float32 [], replicated
All inputs are finite; a program needn't handle non-finite values.
Results may differ from a plain program's by a relative error of at most 0.011.
Values may be sent and summed in bfloat16 or wider, within the bound.
No kernel may reach another device: no remote copies, remote signals or barrier semaphores. Data moves between devices by JAX's collectives and lax.ppermute only.
A program may use at most 128 MiB of HBM per device.

v0:
```python
import jax
import jax.numpy as jnp
from jax import lax
from jax.sharding import PartitionSpec as P

FEAT = 8192


EPSILON = 1e-05
WEIGHT_SCALE = 42.0


def finish_norm(values, sums, clip_count):
    column_mean = sums[0] / clip_count
    scale = lax.rsqrt(sums[1] / clip_count - column_mean * column_mean + EPSILON)
    return (((values - column_mean) * scale).astype(jnp.bfloat16), scale)


def finish_grad(back, normed, moments, scale, clip_count):
    normal_f = normed.astype(jnp.float32)
    return (scale * (back - moments[0] / clip_count - normal_f * (moments[1] / clip_count))).astype(
        jnp.bfloat16
    )


def pick_group(whole, cam_index, cam_count, row_count):
    width = whole.shape[1]
    shaped = whole.reshape(-1, cam_count, row_count, width)
    return lax.dynamic_index_in_dim(shaped, cam_index, 1, keepdims=False).reshape(-1, width)


def on_device(view_a, view_b):
    row_count, width_a = view_a.shape
    width_b = view_b.shape[1]
    cam_count = lax.axis_size("cam")
    cam_index = lax.axis_index("cam")
    clip_count = row_count * lax.axis_size("fc") * cam_count
    values_a = view_a.astype(jnp.float32)
    values_b = view_b.astype(jnp.float32)
    sums_a = lax.psum(
        (jnp.sum(values_a, axis=0), jnp.sum(values_a * values_a, axis=0)), ("fc", "cam")
    )
    sums_b = lax.psum(
        (jnp.sum(values_b, axis=0), jnp.sum(values_b * values_b, axis=0)), ("fr", "cam")
    )
    norm_a, scale_a = finish_norm(values_a, sums_a, clip_count)
    norm_b, scale_b = finish_norm(values_b, sums_b, clip_count)
    contract = (((0,), (0,)), ((), ()))
    whole_a = lax.all_gather(norm_a, ("fc", "cam"), axis=0, tiled=True)
    whole_b = lax.all_gather(norm_b, ("fr", "cam"), axis=0, tiled=True)
    correlation = (
        lax.dot_general(whole_a, whole_b, contract, preferred_element_type=jnp.float32) / clip_count
    )
    group_a = pick_group(whole_a, cam_index, cam_count, row_count)
    group_b = pick_group(whole_b, cam_index, cam_count, row_count)
    row_ids = lax.axis_index("fr") * width_a + lax.broadcasted_iota(
        jnp.int32, (width_a, width_b), 0
    )
    col_ids = lax.axis_index("fc") * width_b + lax.broadcasted_iota(
        jnp.int32, (width_a, width_b), 1
    )
    on_diag = row_ids == col_ids
    weight = WEIGHT_SCALE / FEAT
    missing = 1.0 - correlation
    tile_loss = jnp.sum(jnp.where(on_diag, missing * missing, weight * correlation * correlation))
    loss = lax.psum(tile_loss, ("fr", "fc")) / FEAT
    grad_corr = jnp.where(on_diag, -2.0 * missing, 2.0 * weight * correlation).astype(jnp.bfloat16)
    block_rows = group_b
    back_a = lax.psum_scatter(
        lax.dot_general(
            block_rows, grad_corr, (((1,), (1,)), ((), ())), preferred_element_type=jnp.float32
        ),
        "fc",
        scatter_dimension=0,
        tiled=True,
    )
    block_rows = group_a
    back_b = lax.psum_scatter(
        jnp.dot(block_rows, grad_corr, preferred_element_type=jnp.float32),
        "fr",
        scatter_dimension=0,
        tiled=True,
    )
    normal_a = norm_a.astype(jnp.float32)
    normal_b = norm_b.astype(jnp.float32)
    moments_a = lax.psum(
        (jnp.sum(back_a, axis=0), jnp.sum(back_a * normal_a, axis=0)), ("fc", "cam")
    )
    moments_b = lax.psum(
        (jnp.sum(back_b, axis=0), jnp.sum(back_b * normal_b, axis=0)), ("fr", "cam")
    )
    grad_a = finish_grad(back_a, norm_a, moments_a, scale_a, clip_count)
    grad_b = finish_grad(back_b, norm_b, moments_b, scale_b, clip_count)
    return (grad_a, grad_b, loss)


def solution(mesh):
    in_specs = (P(("fc", "cam"), "fr"), P(("fr", "cam"), "fc"))
    out_specs = (P(("fc", "cam"), "fr"), P(("fr", "cam"), "fc"), P())
    return jax.shard_map(
        on_device, mesh=mesh, in_specs=in_specs, out_specs=out_specs, check_vma=False
    )
```

profile of v0, /device:TPU:0, one launch (start us, length us, event | category | flops | bytes accessed | tf_op | source)
XLA Modules:
  0.0 579.2 jit_solution(1612661345866284545)
XLA Ops:
  7.2 1.2 fusion.10
  8.4 42.5 %all-reduce.1 = (f32[1024]{0:T(1024)S(1)}, f32[1024]{0:T(1024)S(1)}) all-reduce(f32[1024]{0:T(1024)S(1)} %get-tuple-element.10, f32[1024]{0:T(1024)S(1)} %get-tuple-element.9), channel_id=1, replica_groups=mesh['fr'=8,'fc'=8,'cam'=2] {'fc','cam'}, use_global_device_ids=true, to_apply=%region_3.0 | all-reduce | flops 2048 | bytes 16384 | tf_op jit(solution)/shard_map/psum | solution.py:40
  51.0 2.0 fusion.12
  53.0 0.0 all-gather.3.cloned.1.call-start
  53.0 1.2 convert_reduce_fusion
  54.2 40.5 %all-reduce.3 = (f32[1024]{0:T(1024)S(1)}, f32[1024]{0:T(1024)S(1)}) all-reduce(f32[1024]{0:T(1024)S(1)} %get-tuple-element.8, f32[1024]{0:T(1024)S(1)} %get-tuple-element.7), channel_id=1, replica_groups=mesh['fr'=8,'fc'=8,'cam'=2] {'fr','cam'}, use_global_device_ids=true, to_apply=%region_7.0 | all-reduce | flops 2048 | bytes 16384 | tf_op jit(solution)/shard_map/psum | solution.py:43
  94.8 2.0 fusion.14
  96.8 0.0 reduce-scatter.5.cloned.1.call-start
  96.9 136.5 %all-gather.5.cloned.1.call-done = bf16[4096,1024]{1,0:T(8,128)(2,1)} async-done(((bf16[256,1024]{1,0:T(8,128)(2,1)}), bf16[4096,1024]{1,0:T(8,128)(2,1)}) %all-gather.5.cloned.1.call-update) | async-done | bytes 8388624 | tf_op jit(solution)/shard_map/all_gather | solution.py:49
  233.4 4.6 constant_dynamic-slice_fusion
  238.0 72.7 %all-gather.3.cloned.1.call-done = bf16[4096,1024]{1,0:T(8,128)(2,1)} async-done(((bf16[256,1024]{1,0:T(8,128)(2,1)}), bf16[4096,1024]{1,0:T(8,128)(2,1)}) %all-gather.3.cloned.1.call-update) | async-done | bytes 8388624 | tf_op jit(solution)/shard_map/all_gather | solution.py:50
  310.7 15.2 %fusion.1 = (f32[]{:T(128)}, f32[1024,1024]{1,0:T(8,128)S(1)}) fusion(s32[1024]{0:T(1024)S(1)} %get-tuple-element.25, s32[1024]{0:T(1024)S(1)} %get-tuple-element.26, bf16[4096,1024]{1,0:T(8,128)(2,1)} %all-gather.5.cloned.1.call-done, bf16[4096,1024]{1,0:T(8,128)(2,1)} %all-gather.3.cloned.1.call-done), kind=kOutput, calls=%fused_computation.3 | convolution fusion | flops 8598323200 | bytes 20979716 | tf_op jit(solution)/shard_map/dot_general | solution.py:52
  325.9 1.9 copy-done.4
  327.8 7.2 %fusion.16 = f32[2048,1024]{1,0:T(8,128)} fusion(bf16[2048,1024]{1,0:T(8,128)(2,1)S(1)} %bitcast.8, f32[1024,1024]{1,0:T(8,128)S(1)} %get-tuple-element.24, s32[1024]{0:T(1024)S(1)} %get-tuple-element.25, s32[1024]{0:T(1024)S(1)} %get-tuple-element.26), kind=kOutput, calls=%fused_computation.40 | convolution fusion | flops 4302307328 | bytes 16785408 | tf_op jit(solution)/shard_map/dot_general | solution.py:79
  335.1 2.8 constant_dynamic-slice_fusion.1
  337.9 0.6 copy-done.5
  338.5 7.5 %fusion.18 = f32[2048,1024]{1,0:T(8,128)} fusion(bf16[2048,1024]{1,0:T(8,128)(2,1)S(1)} %bitcast.9, f32[1024,1024]{1,0:T(8,128)S(1)} %copy-done.5, s32[1024]{0:T(1024)S(1)} %get-tuple-element.25, s32[1024]{0:T(1024)S(1)} %get-tuple-element.26), kind=kOutput, calls=%fused_computation.41 | convolution fusion | flops 4302307328 | bytes 16785408 | tf_op jit(solution)/shard_map/dot_general | solution.py:70
  346.0 144.9 %psum.71 = f32[]{:T(128)} all-reduce(f32[]{:T(128)} %get-tuple-element.23), channel_id=1, replica_groups=mesh['fr'=8,'fc'=8,'cam'=2] {'fr','fc'}, use_global_device_ids=true, to_apply=%region_19.20 | all-reduce | flops 1 | bytes 8 | tf_op jit(solution)/shard_map/psum | solution.py:66
  491.6 1.5 fusion.20
  493.0 35.7 %all-reduce.2 = (f32[1024]{0:T(1024)S(1)}, f32[1024]{0:T(1024)S(1)}) all-reduce(f32[1024]{0:T(1024)S(1)} %get-tuple-element.4, f32[1024]{0:T(1024)S(1)} %get-tuple-element.3), channel_id=1, replica_groups=mesh['fr'=8,'fc'=8,'cam'=2] {'fr','cam'}, use_global_device_ids=true, to_apply=%region_17.18 | all-reduce | flops 2048 | bytes 16384 | tf_op jit(solution)/shard_map/psum | solution.py:89
  528.8 1.5 fusion.21
  530.4 37.8 %all-reduce = (f32[1024]{0:T(1024)S(1)}, f32[1024]{0:T(1024)S(1)}) all-reduce(f32[1024]{0:T(1024)S(1)} %get-tuple-element.6, f32[1024]{0:T(1024)S(1)} %get-tuple-element.5), channel_id=1, replica_groups=mesh['fr'=8,'fc'=8,'cam'=2] {'fc','cam'}, use_global_device_ids=true, to_apply=%region_12.13 | all-reduce | flops 2048 | bytes 16384 | tf_op jit(solution)/shard_map/psum | solution.py:86
  568.2 2.3 fusion.9
  570.4 1.1 fusion.5
  (25 shorter events, 0.2 us)
Async XLA Ops:
  7.2 226.2 %all-gather.5.cloned.1.call-start = ((), (), s32[]{:S(2)}) async-start(), calls=%async_computation.3 | async-start | bytes 8912896 | tf_op jit(solution)/shard_map/all_gather | solution.py:49
  53.0 257.7 %all-gather.3.cloned.1.call-start = ((), (), s32[]{:S(2)}) async-start(), calls=%async_computation.2 | async-start | bytes 8912896 | tf_op jit(solution)/shard_map/all_gather | solution.py:50
  96.8 394.8 %reduce-scatter.5.cloned.1.call-start = ((), (), s32[]{:S(2)}) async-start(), calls=%async_computation.5 | async-start | bytes 9437184 | tf_op jit(solution)/shard_map/reduce_scatter | solution.py:78
  310.7 17.1 %copy-start.2 = (bf16[8,1,256,1024]{3,2,1,0:T(8,128)(2,1)S(1)}, bf16[8,1,256,1024]{3,2,1,0:T(8,128)(2,1)}, u32[]{:S(2)}) copy-start(bf16[8,1,256,1024]{3,2,1,0:T(8,128)(2,1)} %constant_dynamic-slice_fusion) | copy-start | bytes 12582916
  325.9 1.9 copy-start.4
  335.0 193.8 %reduce-scatter.3.cloned.1.call-start = ((), (), s32[]{:S(2)}) async-start(), calls=%async_computation.4 | async-start | bytes 9437184 | tf_op jit(solution)/shard_map/reduce_scatter | solution.py:69
  335.1 3.5 copy-start.5
  346.0 145.6 %copy-start = (bf16[256,1024]{1,0:T(8,128)(2,1)S(1)}, bf16[256,1024]{1,0:T(8,128)(2,1)}, u32[]{:S(2)}) copy-start(bf16[256,1024]{1,0:T(8,128)(2,1)} %param.3) | copy-start | bytes 1572868
  346.0 182.8 %copy-start.1 = (bf16[256,1024]{1,0:T(8,128)(2,1)S(1)}, bf16[256,1024]{1,0:T(8,128)(2,1)}, u32[]{:S(2)}) copy-start(bf16[256,1024]{1,0:T(8,128)(2,1)} %param.2) | copy-start | bytes 1572868
  528.8 41.6 %copy-start.3 = (f32[256,1024]{1,0:T(8,128)S(1)}, f32[256,1024]{1,0:T(8,128)}, u32[]{:S(2)}) copy-start(f32[256,1024]{1,0:T(8,128)} %reduce-scatter.3.cloned.1.call-done) | copy-start | bytes 3145732
Sparse Core Ops, SparseCore 0:
  53.1 180.2 all-gather.4
  236.4 74.2 all-gather.2
  335.1 50.0 reduce-scatter.4
  387.5 93.9 reduce-scatter.2
where the time goes:
time: 580 us; the launch traced here: 579 us
  blocking collectives  301 us (52%)
  waiting for transfers between devices  209 us (36%)
  matrix products  29.9 us (5%)
  between operations  15.7 us (3%)
  other arithmetic  12.7 us (2%)
  local copies, waits for them, and re-layouts  9.97 us (2%)
    psum x1, blocking collectives, on_device(): loss = lax.psum(tile_loss, ('fr', 'fc')) / FEAT  145 us
    all_gather x1, waiting for transfers between devices, on_device(): whole_a = lax.all_gather(norm_a, ('fc', 'cam'), axis=0, tiled=True)  137 us
    all_gather x1, waiting for transfers between devices, on_device(): whole_b = lax.all_gather(norm_b, ('fr', 'cam'), axis=0, tiled=True)  72.7 us
    psum x1, blocking collectives, on_device(): lax.psum((jnp.sum(values_a, axis=0), jnp.sum(values_a * values_a, axis=0)...  42.5 us
    psum x1, blocking collectives, on_device(): lax.psum((jnp.sum(values_b, axis=0), jnp.sum(values_b * values_b, axis=0)...  40.5 us
    psum x1, blocking collectives, on_device(): lax.psum((jnp.sum(back_a, axis=0), jnp.sum(back_a * normal_a, axis=0)), (...  37.8 us
    psum x1, blocking collectives, on_device(): lax.psum((jnp.sum(back_b, axis=0), jnp.sum(back_b * normal_b, axis=0)), (...  35.7 us
    dot_general x1, matrix products, on_device(): lax.dot_general(whole_a, whole_b, contract, preferred_element_type=jnp.fl...  15.2 us
  transfers between devices with their start and end apart: 4, of which 2 were waited for; matrix products, arithmetic and copies ran while one was open for 3% of the time, Pallas kernels for 0%

commit v1 on v0

v1 whole, which is shorter than its diff:
```python
import functools

import jax
import jax.numpy as jnp
from jax import lax
from jax.experimental import pallas as pl
from jax.experimental.pallas import tpu as pltpu
from jax.sharding import PartitionSpec as P

FEAT = 8192
CLIPS = 4096
EPSILON = 1e-05
WEIGHT = 42.0 / FEAT

AXES = ("fr", "fc", "cam")
BLOCK = 256
HALF_A = 512
WIDE_B = 1024
STEPS = 4
VMEM_LIMIT = 56 * 1024 * 1024


def send(value, move):
    pairs = []
    for device in range(128):
        fr, fc, hi = device // 16, device // 2 % 8, device % 2
        x, core, y, lo, hi = move(fr // 2, fr % 2, fc % 4, fc // 4, hi)
        pairs.append((device, ((x % 4) * 2 + core) * 16 + (lo * 4 + y % 4) * 2 + hi))
    return lax.ppermute(value, AXES, pairs)


def ring_x(value):
    return send(value, lambda x, c, y, lo, hi: (x + 1 - 2 * c, c, y, lo, hi))


def ring_y(value):
    return send(value, lambda x, c, y, lo, hi: (x, c, y + 1 - 2 * c, lo, hi))


def swap_core(value):
    return send(value, lambda x, c, y, lo, hi: (x, 1 - c, y, lo, hi))


def swap_lo(value):
    return send(value, lambda x, c, y, lo, hi: (x, c, y, 1 - lo, hi))


def swap_near(value):
    return send(value, lambda x, c, y, lo, hi: (x, c, y, 1 - lo, 1 - hi))


def half_cam(value, first):
    return send(value, lambda x, c, y, lo, hi: (x, c, y, 1 - lo, hi if c != first else 1 - hi))


def tie(*values):
    return lax.optimization_barrier(values)


class Order:
    def __init__(self, value=None):
        self.last = value

    def __call__(self, value):
        if self.last is not None:
            value, _ = tie(value, self.last)
        self.last = value
        return value


def sublanes(values):
    rows, width = values.shape
    return jnp.sum(values.reshape(rows // 8, 8, width), axis=0)


def lane_groups(values):
    total = values[:, :128]
    for n in range(1, values.shape[1] // 128):
        total = total + values[:, n * 128 : (n + 1) * 128]
    return total


def split_rows(row):
    high = row.astype(jnp.bfloat16).astype(jnp.float32)
    mid = (row - high).astype(jnp.bfloat16).astype(jnp.float32)
    low = row - high - mid
    ids = lax.broadcasted_iota(jnp.int32, (16, row.shape[1]), 0)
    picked = jnp.where(ids == 0, high, jnp.where(ids == 1, mid, jnp.where(ids == 2, low, 0.0)))
    return picked.astype(jnp.bfloat16)


def statistics(ref, width):
    step = 256
    zero = jnp.zeros((8, width), jnp.float32)

    def add(k, carry):
        total, squares = carry
        values = ref[pl.ds(pl.multiple_of(k * step, step), step), :].astype(jnp.float32)
        return total + sublanes(values), squares + sublanes(values * values)

    total, squares = lax.fori_loop(0, CLIPS // step, add, (zero, zero))
    mean = jnp.sum(total, axis=0, keepdims=True) / CLIPS
    msq = jnp.sum(squares, axis=0, keepdims=True) / CLIPS
    return mean, lax.rsqrt(msq - mean * mean + EPSILON)


def normalize_rows(ref, rows, mean, scale):
    normed = ((ref[rows, :].astype(jnp.float32) - mean) * scale).astype(jnp.bfloat16)
    ref[rows, :] = normed
    return sublanes(normed.astype(jnp.float32))


def finish(back, normed, vec):
    back = back - vec[1:2, :] - normed.astype(jnp.float32) * vec[2:3, :]
    return (back * vec[0:1, :]).astype(jnp.bfloat16)


def row_sets(place, bases, k):
    first_a, first_b = place[bases["rows_a"] + k], place[bases["rows_b"] + 2 * k]
    own_b = place[bases["rows_b"] + 2 * k + 1]
    return [pl.multiple_of(start, 512) for start in (first_b, own_b, first_a, first_a + 2048)]


def product(n, place, bases, a_rows, b_rows, grad_ref, vec_a, vec_b, part_a, part_b):
    if n < 2:
        back = jnp.dot(a_rows[...], grad_ref[...], preferred_element_type=jnp.float32)
        value = finish(back, b_rows[...], vec_b)
        part, spots = part_b.at[pl.ds(n * 512, 512)], 4
    else:
        back = lax.dot_general(
            b_rows[...], grad_ref[...], (((1,), (1,)), ((), ())), preferred_element_type=jnp.float32
        )
        value = finish(back, a_rows[...], vec_a)
        part, spots = part_a, 2 * (n - 2)
    for half in range(2):
        spot = pl.multiple_of(place[bases["spot"] + spots + half], BLOCK)
        part[pl.ds(spot, BLOCK), :] = value[half * BLOCK : (half + 1) * BLOCK]
    return part


def front_kernel(plan_a, plan_b, bases, *refs):
    place = refs[0]
    count_a = 1 + max(p for p, *_ in plan_a)
    count_b = 1 + max(p for p, *_ in plan_b)
    pieces_a, pieces_b = refs[1 : 1 + count_a], refs[1 + count_a : 1 + count_a + count_b]
    refs = refs[1 + count_a + count_b :]
    twin, twins = refs[0:2]
    own, leave, stay, owns, leaves, stays, loss_ref = refs[2:9]
    a_ref, b_ref, c_ref, grad_ref, vec_a, vec_b, parts_a, parts_b = refs[9:17]
    sems_a, sems_b, sems_out = refs[17:]

    def copies(plan, pieces, whole, sems, base):
        made = []
        for n, (piece, start, rows, _) in enumerate(plan):
            target = pl.multiple_of(place[base + n], BLOCK)
            made.append(
                pltpu.make_async_copy(
                    pieces[piece].at[pl.ds(start, rows)],
                    whole.at[pl.ds(target, rows)],
                    sems.at[n],
                )
            )
        return made

    moves_a = copies(plan_a, pieces_a, a_ref, sems_a, bases["a"])
    moves_b = copies(plan_b, pieces_b, b_ref, sems_b, bases["b"])
    for move in moves_a + moves_b:
        move.start()
    for move in moves_a:
        move.wait()
    mean_a, scale_a = statistics(a_ref, HALF_A)
    for move in moves_b:
        move.wait()
    mean_b, scale_b = statistics(b_ref, WIDE_B)

    step = 1024
    sums_a = jnp.zeros((8, HALF_A), jnp.float32)
    sums_b = jnp.zeros((8, WIDE_B), jnp.float32)
    for k in range(CLIPS // step):
        rows = pl.ds(k * step, step)
        sums_a += normalize_rows(a_ref, rows, mean_a, scale_a)
        sums_b += normalize_rows(b_ref, rows, mean_b, scale_b)
        part = lax.dot_general(
            a_ref[rows, :],
            b_ref[rows, :],
            (((0,), (0,)), ((), ())),
            preferred_element_type=jnp.float32,
        )
        if k == 0:
            c_ref[...] = part
        else:
            c_ref[...] += part
    mean_a = jnp.sum(sums_a, axis=0, keepdims=True) / CLIPS
    mean_b = jnp.sum(sums_b, axis=0, keepdims=True) / CLIPS

    first_id = place[bases["id"]]
    rows = 128
    zero = jnp.zeros((8, WIDE_B), jnp.float32)
    loss, second_b = zero, zero
    for k in range(HALF_A // rows):
        corr = c_ref[pl.ds(k * rows, rows), :] * (1.0 / CLIPS)
        ids = lax.broadcasted_iota(jnp.int32, (rows, WIDE_B), 0) + (first_id + k * rows)
        on_diag = ids == lax.broadcasted_iota(jnp.int32, (rows, WIDE_B), 1)
        missing = 1.0 - corr
        loss += sublanes(jnp.where(on_diag, missing * missing, WEIGHT * corr * corr))
        grad = jnp.where(on_diag, -2.0 * missing, 2.0 * WEIGHT * corr).astype(jnp.bfloat16)
        grad_ref[pl.ds(k * rows, rows), :] = grad
        second = grad.astype(jnp.float32) * corr
        second_b += sublanes(second)
        vec_a[2:3, pl.ds(k * rows, rows)] = jnp.sum(lane_groups(second).T, axis=0, keepdims=True)
    loss_ref[...] = lane_groups(loss)
    first_a = lax.dot_general(
        split_rows(mean_b),
        grad_ref[...],
        (((1,), (1,)), ((), ())),
        preferred_element_type=jnp.float32,
    )
    first_b = jnp.dot(split_rows(mean_a), grad_ref[...], preferred_element_type=jnp.float32)
    vec_a[0:1, :] = scale_a
    vec_a[1:2, :] = jnp.sum(first_a, axis=0, keepdims=True)
    vec_b[0:1, :] = scale_b
    vec_b[1:2, :] = jnp.sum(first_b, axis=0, keepdims=True)
    vec_b[2:3, :] = jnp.sum(second_b, axis=0, keepdims=True)

    def copies_out(k, targets):
        part_a, part_b = parts_a.at[k], parts_b.at[k]
        sources = [
            part_b.at[pl.ds(0, BLOCK)],
            part_b.at[pl.ds(BLOCK, BLOCK)],
            part_b.at[pl.ds(512, 512)],
            part_a.at[pl.ds(0, 512)],
            part_a.at[pl.ds(512, 512)],
        ]
        return [
            pltpu.make_async_copy(source, target, sems_out.at[5 * k + n])
            for n, (source, target) in enumerate(zip(sources, targets))
        ]

    def run_step(k, start_out):
        for n, start in enumerate(row_sets(place, bases, k)):
            rows = pl.ds(start, 512)
            product(
                n, place, bases, a_ref.at[rows], b_ref.at[rows], grad_ref, vec_a, vec_b,
                parts_a.at[k], parts_b.at[k],
            )
            start_out(n)

    def later_copies(k):
        rows = pl.ds((k - 1) * 512, 512)
        early = k == STEPS - 1
        second = jnp.where(early, 1024, (k - 1) * 512 + BLOCK)
        second = pl.ds(pl.multiple_of(second, BLOCK), BLOCK)
        first = pl.ds(pl.multiple_of(jnp.where(early, 0, (k - 1) * 512), BLOCK), BLOCK)
        targets = [twins.at[first], twins.at[second], owns.at[rows], leaves.at[rows], stays.at[rows]]
        made = copies_out(k, targets)
        return made, copies_out(k, [twin.at[pl.ds(512, BLOCK)]])[0]

    first_copies = copies_out(
        0, [twin.at[pl.ds(0, BLOCK)], twin.at[pl.ds(BLOCK, BLOCK)], own, leave, stay]
    )

    def start_first(n):
        for copy in ((0, 1), (2,), (), (3, 4))[n]:
            first_copies[copy].start()

    run_step(0, start_first)

    def later(k, carry):
        made, early = later_copies(k)

        def start_later(n):
            if n == 0:

                @pl.when(k == STEPS - 1)
                def _():
                    early.start()

                @pl.when(k < STEPS - 1)
                def _():
                    made[0].start()

            for copy in ((1,), (2,), (), (3, 4))[n]:
                made[copy].start()

        run_step(k, start_later)
        return carry

    lax.fori_loop(1, STEPS, later, 0)
    for copy in first_copies:
        copy.wait()
    for k in range(1, STEPS):
        for copy in later_copies(jnp.int32(k))[0]:
            copy.wait()


ANY = pl.BlockSpec(memory_space=pl.ANY)
IN_VMEM = pl.BlockSpec(memory_space=pltpu.VMEM)
NARROW = jax.ShapeDtypeStruct((512, HALF_A), jnp.bfloat16)
WIDE = jax.ShapeDtypeStruct((512, WIDE_B), jnp.bfloat16)


def run_front(place, bases, pieces_a, pieces_b, plan_a, plan_b):
    out = pl.pallas_call(
        functools.partial(front_kernel, plan_a, plan_b, bases),
        out_shape=tuple(
            jax.ShapeDtypeStruct(shape, jnp.bfloat16)
            for shape in (
                (768, WIDE_B),
                (1280, WIDE_B),
                (512, WIDE_B),
                (512, HALF_A),
                (512, HALF_A),
                (1536, WIDE_B),
                (1536, HALF_A),
                (1536, HALF_A),
            )
        )
        + (jax.ShapeDtypeStruct((8, 128), jnp.float32),),
        in_specs=[pl.BlockSpec(memory_space=pltpu.SMEM)]
        + [ANY] * (len(pieces_a) + len(pieces_b)),
        out_specs=(ANY,) * 8 + (IN_VMEM,),
        scratch_shapes=[
            pltpu.VMEM((CLIPS, HALF_A), jnp.bfloat16),
            pltpu.VMEM((CLIPS, WIDE_B), jnp.bfloat16),
            pltpu.VMEM((HALF_A, WIDE_B), jnp.float32),
            pltpu.VMEM((HALF_A, WIDE_B), jnp.bfloat16),
            pltpu.VMEM((8, HALF_A), jnp.float32),
            pltpu.VMEM((8, WIDE_B), jnp.float32),
            pltpu.VMEM((STEPS, 1024, HALF_A), jnp.bfloat16),
            pltpu.VMEM((STEPS, 1024, WIDE_B), jnp.bfloat16),
            pltpu.SemaphoreType.DMA((len(plan_a),)),
            pltpu.SemaphoreType.DMA((len(plan_b),)),
            pltpu.SemaphoreType.DMA((5 * STEPS,)),
        ],
        compiler_params=pltpu.CompilerParams(vmem_limit_bytes=VMEM_LIMIT),
        cost_estimate=pl.CostEstimate(
            flops=6 * CLIPS * HALF_A * WIDE_B, bytes_accessed=24 << 20, transcendentals=0
        ),
        name="front",
    )(place, *pieces_a, *pieces_b)
    parts = [out[2:5]]
    for k in range(STEPS - 1):
        parts.append(tuple(whole[k * 512 : (k + 1) * 512] for whole in out[5:8]))
    return out[0], out[1], parts, out[8]


def add(*parts, to=jnp.bfloat16):
    total = parts[0].astype(jnp.float32)
    for part in parts[1:]:
        total = total + part.astype(jnp.float32)
    return total.astype(to)


def on_device(view_a, view_b):
    fr, fc, hi = lax.axis_index("fr"), lax.axis_index("fc"), lax.axis_index("cam")
    x, core, lo, y = fr // 2, fr % 2, fc // 4, fc % 4
    way = 1 - 2 * core

    left, right = view_a[:, :HALF_A], view_a[:, HALF_A:]
    other = jnp.where(hi == 0, right, left)
    mine = jnp.where(hi == 0, left, right)
    plan_a, plan_b = [], []
    spots = [(lo, hi), (1 - lo, hi), (1 - lo, 1 - hi), (lo, 1 - hi)]
    for n in range(2 * STEPS):
        y_at = (y - n % 4 * way) % 4
        for half in range(2):
            lo_at, hi_at = spots[n // 4 * 2 + half]
            row = ((lo_at * 4 + y_at) * 2 + hi_at) * BLOCK
            plan_a.append((n, half * BLOCK, BLOCK, row))
    for n in range(4 * STEPS):
        group, k = n // 4, n % 4
        core_at = core if group < 2 else 1 - core
        hi_at = hi if group % 2 == 0 else 1 - hi
        x_at = (x - k * (1 - 2 * core_at)) % 4
        plan_b.append((n, 0, BLOCK, ((x_at * 2 + core_at) * 2 + hi_at) * BLOCK))
    order_a = []
    for lo_at in range(2):
        for hi_at in range(2):
            same_lo, same_hi = lo == lo_at, hi == hi_at
            stays = same_lo == same_hi
            order_a.append((stays * 2 + same_lo) * BLOCK)
    order_b = [(hi == 0) * BLOCK, (hi == 1) * BLOCK]
    rows_a, rows_b = [], []
    for k in range(1, STEPS + 1):
        rows_a.append(((y - k * way) % 4) * 512)
        rows_b.append((((x + k * way) % 4) * 2 + 1 - core) * 512)
        rows_b.append((((x - k * way) % 4) * 2 + core) * 512)
    tables = {
        "a": [row for *_, row in plan_a],
        "b": [row for *_, row in plan_b],
        "id": [fr * 1024 + hi * HALF_A - fc * WIDE_B],
        "spot": order_a + order_b,
        "rows_a": rows_a,
        "rows_b": rows_b,
    }
    bases, flat = {}, []
    for name, table in tables.items():
        bases[name] = len(flat)
        flat += [jnp.asarray(value, jnp.int32) for value in table]
    place = jnp.stack(flat)

    then = Order()
    partner = half_cam(view_b, True)
    b_1, twin_0 = ring_x(view_b), swap_core(view_b)
    from_near = swap_near(other)
    from_lo = swap_lo(mine)
    partner = then(partner)
    partner = half_cam(partner, False)
    from_near = then(from_near)
    from_far = swap_lo(from_near)
    from_lo = then(from_lo)
    a_0 = jnp.concatenate([mine, from_lo], axis=0)
    a_1 = ring_y(a_0)
    b_1 = then(b_1)
    b_2, twin_1 = ring_x(b_1), swap_core(b_1)
    twin_0 = then(twin_0)
    partner = then(partner)
    partner_1, twin_4 = ring_x(partner), swap_core(partner)
    from_far = then(from_far)
    others_0 = jnp.concatenate([from_near, from_far], axis=0)
    others_1 = ring_y(others_0)
    a_1 = then(a_1)
    a_2 = ring_y(a_1)
    b_2 = then(b_2)
    b_3, twin_2 = ring_x(b_2), swap_core(b_2)
    twin_1 = then(twin_1)
    partner_1 = then(partner_1)
    partner_2, twin_5 = ring_x(partner_1), swap_core(partner_1)
    others_1 = then(others_1)
    others_2 = ring_y(others_1)
    twin_4 = then(twin_4)
    a_2 = then(a_2)
    a_3 = ring_y(a_2)
    twin_2 = then(twin_2)
    place = then(place)
    b_3 = then(b_3)
    twin_3 = swap_core(b_3)
    partner_2 = then(partner_2)
    partner_3, twin_6 = ring_x(partner_2), swap_core(partner_2)
    others_2 = then(others_2)
    others_3 = ring_y(others_2)
    twin_5 = then(twin_5)
    a_3 = then(a_3)
    twin_3 = then(twin_3)
    twin_6 = then(twin_6)
    partner_3 = then(partner_3)
    twin_7 = swap_core(partner_3)
    others_3 = then(others_3)
    pieces_a = [a_0, a_1, a_2, a_3, others_0, others_1, others_2, others_3]
    pieces_b = [view_b, b_1, b_2, b_3, partner, partner_1, partner_2, partner_3]
    pieces_b += [twin_0, twin_1, twin_2, twin_3, twin_4, twin_5, twin_6, twin_7]

    twin, twins, parts, loss = run_front(place, bases, pieces_a, pieces_b, plan_a, plan_b)

    def total(value, hop):
        return value + hop(value)

    own, leave, stay = parts[0]
    twin = swap_core(twin)
    loss = total(loss, swap_lo)
    then = Order(loss)
    twin = then(twin)
    twins, _ = tie(twins, twin)
    twins = swap_core(twins)
    cross = add(own[:BLOCK], twin[:BLOCK])
    then.last = cross
    keep = add(own[BLOCK:], then(twin)[BLOCK:512])
    then.last = keep
    far = add(parts[STEPS - 1][0][:BLOCK], then(twin)[512:])
    then.last = far
    far = half_cam(far, True)
    last = parts[STEPS - 1]

    def chunk(k, rows):
        return parts[k][0][rows], then(twins)[(k - 1) * 512 : k * 512][rows]

    def hop(loss, move):
        loss, _ = tie(loss, then.last)
        loss = total(loss, move)
        then.last = loss
        return loss

    on, end = slice(BLOCK), slice(BLOCK, None)
    for k in (1, 2):
        cross, leave, keep, stay = ring_x(cross), ring_y(leave), ring_x(keep), ring_y(stay)
        if k == 1:
            loss = hop(loss, swap_core)
        cross = add(*chunk(k, on), then(cross))
        then.last = cross
        far = half_cam(then(far), False) if k == 1 else then(far)
        leave = add(parts[k][1], then(leave))
        then.last = leave
        if k == 1:
            keep = add(*chunk(k, end), then(keep))
            then.last = keep
            stay = add(parts[k][2], then(stay))
            then.last = stay
    cross = half_cam(cross, True)
    leave = ring_y(leave)
    keep = add(*chunk(2, end), then(keep), to=jnp.float32)
    then.last = keep
    stay = add(parts[2][2], then(stay))
    then.last = stay
    stay = ring_y(stay)
    loss = hop(loss, swap_near)
    cross = then(cross)
    cross = half_cam(cross, False)
    leave = then(leave)
    leave_on, leave_end = add(last[1][end], leave[end]), add(last[1][on], leave[on])
    arrived_on, arrived_end = swap_lo(leave_on), swap_lo(leave_end)
    then.last = leave_end
    loss = hop(loss, ring_x)
    stay = then(stay)
    loss = hop(loss, lambda value: send(value, lambda x, c, y, lo, hi: (x + 2, c, y, lo, hi)))
    near = add(last[2][on], stay[on], then(arrived_on))
    across = swap_near(near)
    then.last = near
    keep = add(keep, then(cross))
    then.last = keep
    keep = ring_x(keep)
    loss = hop(loss, ring_y)
    arrived_end = then(arrived_end)
    stays = add(last[2][end], stay[end], arrived_end)
    loss = hop(loss, lambda value: send(value, lambda x, c, y, lo, hi: (x, c, y + 2, lo, hi)))
    kept = add(last[0][end], then(twins)[1024:], far, to=jnp.float32)
    grad_a = jnp.where(
        hi == 0,
        jnp.concatenate([stays, across], axis=1),
        jnp.concatenate([across, stays], axis=1),
    )
    grad_b = add(kept, keep)
    return (grad_a, grad_b, jnp.sum(loss) / FEAT)


def solution(mesh):
    in_specs = (P(("fc", "cam"), "fr"), P(("fr", "cam"), "fc"))
    out_specs = (P(("fc", "cam"), "fr"), P(("fr", "cam"), "fc"), P())
    return jax.shard_map(
        on_device, mesh=mesh, in_specs=in_specs, out_specs=out_specs, check_vma=False
    )
```

time: 580 us -> 172 us (0.30)
  blocking collectives: 301 us -> 0 us
  waiting for transfers between devices: 209 us -> 71.9 us
  starting transfers between devices: 0.16 us -> 51.7 us
  matrix products: 29.9 us -> 0 us
  Pallas kernels: 0 us -> 28.4 us
  between operations: 15.7 us -> 2.86 us
  local copies, waits for them, and re-layouts: 9.97 us -> 2.9 us
    psum x5 -> x0, blocking collectives: 301 us -> none  [the longest x1 145 us: on_device(): loss = lax.psum(tile_loss, ('fr', 'fc')) / FEAT]
    all_gather x2 -> x0, waiting for transfers between devices: 209 us -> none  [the longest x1 137 us: on_device(): whole_a = lax.all_gather(norm_a, ('fc', 'cam'), axis=0, tiled=True)]
    ppermute x0 -> x52, waiting for transfers between devices: none -> 71.9 us  [send(): return lax.ppermute(value, AXES, pairs)]
    ppermute x0 -> x52, starting transfers between devices: none -> 51.7 us  [send(): return lax.ppermute(value, AXES, pairs)]
    dot_general x3 -> x0, matrix products: 29.9 us -> none  [the longest x1 15.2 us: on_device(): lax.dot_general(whole_a, whole_b, contract, preferred_element_type=jnp.fl...]
    pallas_call x0 -> x1, Pallas kernels: none -> 28.4 us  [run_front(): pl.pallas_call(functools.partial(front_kernel, plan_a, plan_b, bases), ou...]
    dynamic_slice x2 -> x0, local copies, waits for them, and re-layouts: 7.4 us -> none  [pick_group(): lax.dynamic_index_in_dim(shaped, cam_index, 1, keepdims=False)]
  transfers between devices with their start and end apart: 4 -> 52, of which waited for: 2 -> 27; matrix products, arithmetic and copies ran while one was open for 3% -> 6% of each run, Pallas kernels for 0% -> 0%
where the time goes in v1:
time: 172 us; the launch traced here: 169 us
  waiting for transfers between devices  71.9 us (42%)
  starting transfers between devices  51.7 us (30%)
  Pallas kernels  28.4 us (17%)
  other arithmetic  11.4 us (7%)
  local copies, waits for them, and re-layouts  2.9 us (2%)
  between operations  2.86 us (2%)
    ppermute x52, waiting for transfers between devices, send(): return lax.ppermute(value, AXES, pairs)  71.9 us
    ppermute x52, starting transfers between devices, send(): return lax.ppermute(value, AXES, pairs)  51.7 us
    pallas_call x1, Pallas kernels, run_front(): pl.pallas_call(functools.partial(front_kernel, plan_a, plan_b, bases), ou...  28.4 us
    convert_element_type x15, other arithmetic, add(): return total.astype(to)  7.79 us
  transfers between devices with their start and end apart: 52, of which 27 were waited for; matrix products, arithmetic and copies ran while one was open for 6% of the time, Pallas kernels for 0%

profile of v1, /device:TPU:0, one launch (start us, length us, event | category | flops | bytes accessed | tf_op | source)
XLA Modules:
  0.0 169.1 jit_solution(8730338100345050443)
XLA Ops:
  0.6 2.1 %collective-permute-start.3 = (bf16[256,1024]{1,0:T(8,128)(2,1)}, bf16[256,1024]{1,0:T(8,128)(2,1)}, u32[]{:S(2)}, u32[]{:S(2)}) collective-permute-start(bf16[256,1024]{1,0:T(8,128)(2,1)} %refs_9_.1), channel_id=1, source_target_pairs={{0,8},{1,9},{2,10},{3,11},{4,12},{5,13},{6,14},{7,15},{8,0},{9,1},... | collective-permute-start | bytes 1572872 | tf_op jit(solution)/shard_map/ppermute | solution.py:29
  3.8 2.6 %collective-permute-start.2 = (bf16[256,512]{1,0:T(8,128)(2,1)S(1)}, bf16[256,512]{1,0:T(8,128)(2,1)S(1)}, u32[]{:S(2)}, u32[]{:S(2)}) collective-permute-start(bf16[256,512]{1,0:T(8,128)(2,1)S(1)} %get-tuple-element.135), channel_id=1, source_target_pairs={{0,9},{1,8},{2,11},{3,10},{4,13},{5,12},{6,15},{7,14},{8,1},{9,0},... | collective-permute-start | bytes 786440 | tf_op jit(solution)/shard_map/ppermute | solution.py:29
  8.9 5.4 %collective-permute-done.2 = bf16[256,512]{1,0:T(8,128)(2,1)S(1)} collective-permute-done((bf16[256,512]{1,0:T(8,128)(2,1)S(1)}, bf16[256,512]{1,0:T(8,128)(2,1)S(1)}, u32[]{:S(2)}, u32[]{:S(2)}) %collective-permute-start.2) | collective-permute-done | bytes 262176 | tf_op jit(solution)/shard_map/ppermute | solution.py:29
  15.7 4.1 %collective-permute-start.7 = (bf16[256,1024]{1,0:T(8,128)(2,1)}, bf16[256,1024]{1,0:T(8,128)(2,1)S(1)}, u32[]{:S(2)}, u32[]{:S(2)}) collective-permute-start(bf16[256,1024]{1,0:T(8,128)(2,1)} %collective-permute-done.3), channel_id=1, source_target_pairs={{0,9},{1,8},{2,11},{3,10},{4,13},{5,12},{6,15},{7,14},{8,1},{9,0},... | collective-permute-start | bytes 1572872 | tf_op jit(solution)/shard_map/ppermute | solution.py:29
  23.2 4.0 %collective-permute-done.7.refs_13_ = bf16[256,1024]{1,0:T(8,128)(2,1)S(1)} collective-permute-done((bf16[256,1024]{1,0:T(8,128)(2,1)}, bf16[256,1024]{1,0:T(8,128)(2,1)S(1)}, u32[]{:S(2)}, u32[]{:S(2)}) %collective-permute-start.7) | collective-permute-done | bytes 524320 | tf_op jit(solution)/shard_map/ppermute | solution.py:29
  28.7 2.1 %collective-permute-done.6 = bf16[256,512]{1,0:T(8,128)(2,1)S(1)} collective-permute-done((bf16[256,512]{1,0:T(8,128)(2,1)S(1)}, bf16[256,512]{1,0:T(8,128)(2,1)S(1)}, u32[]{:S(2)}, u32[]{:S(2)}) %collective-permute-start.6) | collective-permute-done | bytes 262176 | tf_op jit(solution)/shard_map/ppermute | solution.py:29
  34.7 3.1 %collective-permute-done.13.refs_14_ = bf16[256,1024]{1,0:T(8,128)(2,1)} collective-permute-done((bf16[256,1024]{1,0:T(8,128)(2,1)S(1)}, bf16[256,1024]{1,0:T(8,128)(2,1)}, u32[]{:S(2)}, u32[]{:S(2)}) %collective-permute-start.13) | collective-permute-done | bytes 524320 | tf_op jit(solution)/shard_map/ppermute | solution.py:29
  38.1 3.3 %collective-permute-done.12.refs_6_ = bf16[512,512]{1,0:T(8,128)(2,1)} collective-permute-done((bf16[512,512]{1,0:T(8,128)(2,1)S(1)}, bf16[512,512]{1,0:T(8,128)(2,1)}, u32[]{:S(2)}, u32[]{:S(2)}) %collective-permute-start.12) | collective-permute-done | bytes 524320 | tf_op jit(solution)/shard_map/ppermute | solution.py:29
  44.7 2.3 %collective-permute-done.10.refs_3_ = bf16[512,512]{1,0:T(8,128)(2,1)} collective-permute-done((bf16[512,512]{1,0:T(8,128)(2,1)S(1)}, bf16[512,512]{1,0:T(8,128)(2,1)}, u32[]{:S(2)}, u32[]{:S(2)}) %collective-permute-start.10) | collective-permute-done | bytes 524320 | tf_op jit(solution)/shard_map/ppermute | solution.py:29
  49.1 5.1 %collective-permute-done.18.refs_15_ = bf16[256,1024]{1,0:T(8,128)(2,1)} collective-permute-done((bf16[256,1024]{1,0:T(8,128)(2,1)}, bf16[256,1024]{1,0:T(8,128)(2,1)}, u32[]{:S(2)}, u32[]{:S(2)}) %collective-permute-start.18) | collective-permute-done | bytes 524320 | tf_op jit(solution)/shard_map/ppermute | solution.py:29
  55.9 4.0 %collective-permute-done.15.refs_4_ = bf16[512,512]{1,0:T(8,128)(2,1)S(1)} collective-permute-done((bf16[512,512]{1,0:T(8,128)(2,1)}, bf16[512,512]{1,0:T(8,128)(2,1)S(1)}, u32[]{:S(2)}, u32[]{:S(2)}) %collective-permute-start.15) | collective-permute-done | bytes 524320 | tf_op jit(solution)/shard_map/ppermute | solution.py:29
  59.9 5.1 %collective-permute-done.21.refs_16_ = bf16[256,1024]{1,0:T(8,128)(2,1)S(1)} collective-permute-done((bf16[256,1024]{1,0:T(8,128)(2,1)}, bf16[256,1024]{1,0:T(8,128)(2,1)S(1)}, u32[]{:S(2)}, u32[]{:S(2)}) %collective-permute-start.21) | collective-permute-done | bytes 524320 | tf_op jit(solution)/shard_map/ppermute | solution.py:29
  68.1 28.4 %front.1 = (bf16[768,1024]{1,0:T(8,128)(2,1)}, bf16[1280,1024]{1,0:T(8,128)(2,1)}, bf16[512,1024]{1,0:T(8,128)(2,1)}, bf16[512,512]{1,0:T(8,128)(2,1)}, bf16[512...) custom-call(s32[51]{0:T(128)} %stack.207.refs_0_, ...), custom_call_target="tpu_custom_call" | custom-call | flops 12884901888 | bytes 25165824 | tf_op jit(solution)/shard_map/front/pallas_call | solution.py:303
  98.2 2.3 %collective-permute-done.27 = f32[8,128]{1,0:T(8,128)S(1)} collective-permute-done((f32[8,128]{1,0:T(8,128)}, f32[8,128]{1,0:T(8,128)S(1)}, u32[]{:S(2)}, u32[]{:S(2)}) %collective-permute-start.27) | collective-permute-done | bytes 4128 | tf_op jit(solution)/shard_map/ppermute | solution.py:29
  107.2 2.9 %collective-permute-start.31 = (f32[8,128]{1,0:T(8,128)S(1)}, f32[8,128]{1,0:T(8,128)S(1)}, u32[]{:S(2)}, u32[]{:S(2)}) collective-permute-start(f32[8,128]{1,0:T(8,128)S(1)} %add.461), channel_id=1, source_target_pairs={{0,16},{1,17},{2,18},{3,19},{4,20},{5,21},{6,22},{7,23},{8,24},{9,... | collective-permute-start | bytes 12296 | tf_op jit(solution)/shard_map/ppermute | solution.py:29
  117.8 3.9 %collective-permute-done.33 = bf16[256,1024]{1,0:T(8,128)(2,1)S(1)} collective-permute-done((bf16[256,1024]{1,0:T(8,128)(2,1)S(1)}, bf16[256,1024]{1,0:T(8,128)(2,1)S(1)}, u32[]{:S(2)}, u32[]{:S(2)}) %collective-permute-start.33) | collective-permute-done | bytes 524320 | tf_op jit(solution)/shard_map/ppermute | solution.py:29
  122.7 4.6 %collective-permute-done.37 = bf16[256,1024]{1,0:T(8,128)(2,1)S(1)} collective-permute-done((bf16[256,1024]{1,0:T(8,128)(2,1)S(1)}, bf16[256,1024]{1,0:T(8,128)(2,1)S(1)}, u32[]{:S(2)}, u32[]{:S(2)}) %collective-permute-start.37) | collective-permute-done | bytes 524320 | tf_op jit(solution)/shard_map/ppermute | solution.py:29
  128.5 4.4 %collective-permute-done.38 = bf16[256,1024]{1,0:T(8,128)(2,1)S(1)} collective-permute-done((bf16[256,1024]{1,0:T(8,128)(2,1)S(1)}, bf16[256,1024]{1,0:T(8,128)(2,1)S(1)}, u32[]{:S(2)}, u32[]{:S(2)}) %collective-permute-start.38) | collective-permute-done | bytes 524320 | tf_op jit(solution)/shard_map/ppermute | solution.py:29
  134.7 3.8 %collective-permute-done.40 = f32[8,128]{1,0:T(8,128)S(1)} collective-permute-done((f32[8,128]{1,0:T(8,128)S(1)}, f32[8,128]{1,0:T(8,128)S(1)}, u32[]{:S(2)}, u32[]{:S(2)}) %collective-permute-start.40) | collective-permute-done | bytes 4128 | tf_op jit(solution)/shard_map/ppermute | solution.py:29
  141.5 3.8 %collective-permute-done.43 = f32[8,128]{1,0:T(8,128)S(1)} collective-permute-done((f32[8,128]{1,0:T(8,128)S(1)}, f32[8,128]{1,0:T(8,128)S(1)}, u32[]{:S(2)}, u32[]{:S(2)}) %collective-permute-start.43) | collective-permute-done | bytes 4128 | tf_op jit(solution)/shard_map/ppermute | solution.py:29
  145.3 2.1 %collective-permute-start.45 = (f32[8,128]{1,0:T(8,128)S(1)}, f32[8,128]{1,0:T(8,128)S(1)}, u32[]{:S(2)}, u32[]{:S(2)}) collective-permute-start(f32[8,128]{1,0:T(8,128)S(1)} %add.480), channel_id=1, source_target_pairs={{0,64},{1,65},{2,66},{3,67},{4,68},{5,69},{6,70},{7,71},{8,72},{9,... | collective-permute-start | bytes 12296 | tf_op jit(solution)/shard_map/ppermute | solution.py:29
  154.8 3.2 %collective-permute-done.48 = f32[8,128]{1,0:T(8,128)S(1)} collective-permute-done((f32[8,128]{1,0:T(8,128)S(1)}, f32[8,128]{1,0:T(8,128)S(1)}, u32[]{:S(2)}, u32[]{:S(2)}) %collective-permute-start.48) | collective-permute-done | bytes 4128 | tf_op jit(solution)/shard_map/ppermute | solution.py:29
  158.0 2.9 %collective-permute-start.50 = (f32[8,128]{1,0:T(8,128)S(1)}, f32[8,128]{1,0:T(8,128)S(1)}, u32[]{:S(2)}, u32[]{:S(2)}) collective-permute-start(f32[8,128]{1,0:T(8,128)S(1)} %add.487), channel_id=1, source_target_pairs={{0,4},{1,5},{2,6},{3,7},{4,0},{5,1},{6,2},{7,3},{8,12},{9,13},{10,... | collective-permute-start | bytes 12296 | tf_op jit(solution)/shard_map/ppermute | solution.py:29
  165.5 2.5 %add_convert_fusion = bf16[256,1024]{1,0:T(8,128)(2,1)} fusion(bf16[256,1024]{1,0:T(8,128)(2,1)} %collective-permute-done.51, bf16[256,1024]{1,0:T(8,128)(2,1)} %copy-done.4, bf16[1280,1024]{1,0:T(8,128)(2,1)} %copy-done.1, bf16[1536,1024]{1,0:T(8,128)(2,1)S(1)} %copy-done), kind=kLoop, calls=%fused_computation | loop fusion | flops 2097152 | bytes 2621440 | tf_op jit(solution)/shard_map/convert_element_type | solution.py:351
  (154 shorter events, 58.3 us)
Async XLA Ops:
  0.6 13.7 %collective-permute-start.3 = (bf16[256,1024]{1,0:T(8,128)(2,1)}, bf16[256,1024]{1,0:T(8,128)(2,1)}, u32[]{:S(2)}, u32[]{:S(2)}) collective-permute-start(bf16[256,1024]{1,0:T(8,128)(2,1)} %refs_9_.1), channel_id=1, source_target_pairs={{0,8},{1,9},{2,10},{3,11},{4,12},{5,13},{6,14},{7,15},{8,0},{9,1},... | collective-permute-start | bytes 1572872 | tf_op jit(solution)/shard_map/ppermute | solution.py:29
  7.4 14.1 %collective-permute-start = (bf16[256,1024]{1,0:T(8,128)(2,1)}, bf16[256,1024]{1,0:T(8,128)(2,1)S(1)}, u32[]{:S(2)}, u32[]{:S(2)}) collective-permute-start(bf16[256,1024]{1,0:T(8,128)(2,1)} %refs_9_.1), channel_id=1, source_target_pairs={{0,32},{1,33},{2,34},{3,35},{4,36},{5,37},{6,38},{7,39},{8,40},{9,... | collective-permute-start | bytes 1572872 | tf_op jit(solution)/shard_map/ppermute | solution.py:29
  8.9 12.7 %collective-permute-start.8 = (bf16[256,1024]{1,0:T(8,128)(2,1)}, bf16[256,1024]{1,0:T(8,128)(2,1)S(1)}, u32[]{:S(2)}, u32[]{:S(2)}) collective-permute-start(bf16[256,1024]{1,0:T(8,128)(2,1)} %refs_9_.1), channel_id=1, source_target_pairs={{0,16},{1,17},{2,18},{3,19},{4,20},{5,21},{6,22},{7,23},{8,24},{9,... | collective-permute-start | bytes 1572872 | tf_op jit(solution)/shard_map/ppermute | solution.py:29
  15.7 11.5 %collective-permute-start.7 = (bf16[256,1024]{1,0:T(8,128)(2,1)}, bf16[256,1024]{1,0:T(8,128)(2,1)S(1)}, u32[]{:S(2)}, u32[]{:S(2)}) collective-permute-start(bf16[256,1024]{1,0:T(8,128)(2,1)} %collective-permute-done.3), channel_id=1, source_target_pairs={{0,9},{1,8},{2,11},{3,10},{4,13},{5,12},{6,15},{7,14},{8,1},{9,0},... | collective-permute-start | bytes 1572872 | tf_op jit(solution)/shard_map/ppermute | solution.py:29
  19.9 12.6 %collective-permute-start.5 = (bf16[512,512]{1,0:T(8,128)(2,1)S(1)}, bf16[512,512]{1,0:T(8,128)(2,1)S(1)}, u32[]{:S(2)}, u32[]{:S(2)}) collective-permute-start(bf16[512,512]{1,0:T(8,128)(2,1)S(1)} %pad_maximum_fusion.refs_1_), channel_id=1, source_target_pairs={{0,2},{1,3},{2,4},{3,5},{4,6},{5,7},{6,0},{7,1},{8,10},{9,11},{10,... | collective-permute-start | bytes 1572872 | tf_op jit(solution)/shard_map/ppermute | solution.py:29
  21.5 12.3 %collective-permute-start.14 = (bf16[256,1024]{1,0:T(8,128)(2,1)S(1)}, bf16[256,1024]{1,0:T(8,128)(2,1)S(1)}, u32[]{:S(2)}, u32[]{:S(2)}) collective-permute-start(bf16[256,1024]{1,0:T(8,128)(2,1)S(1)} %collective-permute-done.refs_10_), channel_id=1, source_target_pairs={{0,16},{1,17},{2,18},{3,19},{4,20},{5,21},{6,22},{7,23},{8,24},{9,... | collective-permute-start | bytes 1572872 | tf_op jit(solution)/shard_map/ppermute | solution.py:29
  21.7 12.2 %collective-permute-start.4 = (bf16[256,1024]{1,0:T(8,128)(2,1)S(1)}, bf16[256,1024]{1,0:T(8,128)(2,1)}, u32[]{:S(2)}, u32[]{:S(2)}) collective-permute-start(bf16[256,1024]{1,0:T(8,128)(2,1)S(1)} %collective-permute-done.refs_10_), channel_id=1, source_target_pairs={{0,32},{1,33},{2,34},{3,35},{4,36},{5,37},{6,38},{7,39},{8,40},{9,... | collective-permute-start | bytes 1572872 | tf_op jit(solution)/shard_map/ppermute | solution.py:29
  33.8 13.2 %collective-permute-start.10 = (bf16[512,512]{1,0:T(8,128)(2,1)S(1)}, bf16[512,512]{1,0:T(8,128)(2,1)}, u32[]{:S(2)}, u32[]{:S(2)}) collective-permute-start(bf16[512,512]{1,0:T(8,128)(2,1)S(1)} %collective-permute-done.5.refs_2_), channel_id=1, source_target_pairs={{0,2},{1,3},{2,4},{3,5},{4,6},{5,7},{6,0},{7,1},{8,10},{9,11},{10,... | collective-permute-start | bytes 1572872 | tf_op jit(solution)/shard_map/ppermute | solution.py:29
  33.9 13.4 %collective-permute-start.9 = (bf16[256,1024]{1,0:T(8,128)(2,1)}, bf16[256,1024]{1,0:T(8,128)(2,1)}, u32[]{:S(2)}, u32[]{:S(2)}) collective-permute-start(bf16[256,1024]{1,0:T(8,128)(2,1)} %collective-permute-done.4.refs_11_), channel_id=1, source_target_pairs={{0,16},{1,17},{2,18},{3,19},{4,20},{5,21},{6,22},{7,23},{8,24},{9,... | collective-permute-start | bytes 1572872 | tf_op jit(solution)/shard_map/ppermute | solution.py:29
  41.4 12.8 %collective-permute-start.18 = (bf16[256,1024]{1,0:T(8,128)(2,1)}, bf16[256,1024]{1,0:T(8,128)(2,1)}, u32[]{:S(2)}, u32[]{:S(2)}) collective-permute-start(bf16[256,1024]{1,0:T(8,128)(2,1)} %collective-permute-done.13.refs_14_), channel_id=1, source_target_pairs={{0,32},{1,33},{2,34},{3,35},{4,36},{5,37},{6,38},{7,39},{8,40},{9,... | collective-permute-start | bytes 1572872 | tf_op jit(solution)/shard_map/ppermute | solution.py:29
  47.2 12.7 %collective-permute-start.15 = (bf16[512,512]{1,0:T(8,128)(2,1)}, bf16[512,512]{1,0:T(8,128)(2,1)S(1)}, u32[]{:S(2)}, u32[]{:S(2)}) collective-permute-start(bf16[512,512]{1,0:T(8,128)(2,1)} %collective-permute-done.10.refs_3_), channel_id=1, source_target_pairs={{0,2},{1,3},{2,4},{3,5},{4,6},{5,7},{6,0},{7,1},{8,10},{9,11},{10,... | collective-permute-start | bytes 1572872 | tf_op jit(solution)/shard_map/ppermute | solution.py:29
  48.6 11.4 %collective-permute-start.23 = (bf16[256,1024]{1,0:T(8,128)(2,1)}, bf16[256,1024]{1,0:T(8,128)(2,1)S(1)}, u32[]{:S(2)}, u32[]{:S(2)}) collective-permute-start(bf16[256,1024]{1,0:T(8,128)(2,1)} %collective-permute-done.19.refs_12_), channel_id=1, source_target_pairs={{0,16},{1,17},{2,18},{3,19},{4,20},{5,21},{6,22},{7,23},{8,24},{9,... | collective-permute-start | bytes 1572872 | tf_op jit(solution)/shard_map/ppermute | solution.py:29
  111.0 11.1 %collective-permute-start.25 = (bf16[512,512]{1,0:T(8,128)(2,1)S(1)}, bf16[512,512]{1,0:T(8,128)(2,1)S(1)}, u32[]{:S(2)}, u32[]{:S(2)}) collective-permute-start(bf16[512,512]{1,0:T(8,128)(2,1)S(1)} %copy-done.13), channel_id=1, source_target_pairs={{0,2},{1,3},{2,4},{3,5},{4,6},{5,7},{6,0},{7,1},{8,10},{9,11},{10,... | collective-permute-start | bytes 1572872 | tf_op jit(solution)/shard_map/ppermute | solution.py:29
  113.2 14.1 %collective-permute-start.37 = (bf16[256,1024]{1,0:T(8,128)(2,1)S(1)}, bf16[256,1024]{1,0:T(8,128)(2,1)S(1)}, u32[]{:S(2)}, u32[]{:S(2)}) collective-permute-start(bf16[256,1024]{1,0:T(8,128)(2,1)S(1)} %add_convert_fusion.8), channel_id=1, source_target_pairs={{0,32},{1,33},{2,34},{3,35},{4,36},{5,37},{6,38},{7,39},{8,40},{9,... | collective-permute-start | bytes 1572872 | tf_op jit(solution)/shard_map/ppermute | solution.py:29
  114.4 13.2 %collective-permute-start.36 = (bf16[256,1024]{1,0:T(8,128)(2,1)S(1)}, bf16[256,1024]{1,0:T(8,128)(2,1)S(1)}, u32[]{:S(2)}, u32[]{:S(2)}) collective-permute-start(bf16[256,1024]{1,0:T(8,128)(2,1)S(1)} %collective-permute-done.30), channel_id=1, source_target_pairs={{0,9},{1,8},{2,11},{3,10},{4,13},{5,12},{6,15},{7,14},{8,1},{9,0},... | collective-permute-start | bytes 1572872 | tf_op jit(solution)/shard_map/ppermute | solution.py:29
  116.2 11.5 %collective-permute-start.35 = (bf16[512,512]{1,0:T(8,128)(2,1)S(1)}, bf16[512,512]{1,0:T(8,128)(2,1)S(1)}, u32[]{:S(2)}, u32[]{:S(2)}) collective-permute-start(bf16[512,512]{1,0:T(8,128)(2,1)S(1)} %add_convert_fusion.7), channel_id=1, source_target_pairs={{0,2},{1,3},{2,4},{3,5},{4,6},{5,7},{6,0},{7,1},{8,10},{9,11},{10,... | collective-permute-start | bytes 1572872 | tf_op jit(solution)/shard_map/ppermute | solution.py:29
  121.9 11.0 %collective-permute-start.38 = (bf16[256,1024]{1,0:T(8,128)(2,1)S(1)}, bf16[256,1024]{1,0:T(8,128)(2,1)S(1)}, u32[]{:S(2)}, u32[]{:S(2)}) collective-permute-start(bf16[256,1024]{1,0:T(8,128)(2,1)S(1)} %add_convert_fusion.6), channel_id=1, source_target_pairs={{0,32},{1,33},{2,34},{3,35},{4,36},{5,37},{6,38},{7,39},{8,40},{9,... | collective-permute-start | bytes 1572872 | tf_op jit(solution)/shard_map/ppermute | solution.py:29
  122.2 11.0 %collective-permute-start.34 = (bf16[512,512]{1,0:T(8,128)(2,1)S(1)}, bf16[512,512]{1,0:T(8,128)(2,1)S(1)}, u32[]{:S(2)}, u32[]{:S(2)}) collective-permute-start(bf16[512,512]{1,0:T(8,128)(2,1)S(1)} %add_convert_fusion.5), channel_id=1, source_target_pairs={{0,2},{1,3},{2,4},{3,5},{4,6},{5,7},{6,0},{7,1},{8,10},{9,11},{10,... | collective-permute-start | bytes 1572872 | tf_op jit(solution)/shard_map/ppermute | solution.py:29
  127.6 11.0 %collective-permute-start.42 = (bf16[256,1024]{1,0:T(8,128)(2,1)S(1)}, bf16[256,1024]{1,0:T(8,128)(2,1)S(1)}, u32[]{:S(2)}, u32[]{:S(2)}) collective-permute-start(bf16[256,1024]{1,0:T(8,128)(2,1)S(1)} %add_convert_fusion.4), channel_id=1, source_target_pairs={{0,8},{1,9},{2,10},{3,11},{4,12},{5,13},{6,14},{7,15},{8,0},{9,1},... | collective-permute-start | bytes 1572872 | tf_op jit(solution)/shard_map/ppermute | solution.py:29
  127.8 11.7 %collective-permute-start.41 = (bf16[512,512]{1,0:T(8,128)(2,1)S(1)}, bf16[512,512]{1,0:T(8,128)(2,1)S(1)}, u32[]{:S(2)}, u32[]{:S(2)}) collective-permute-start(bf16[512,512]{1,0:T(8,128)(2,1)S(1)} %add_convert_fusion.3), channel_id=1, source_target_pairs={{0,2},{1,3},{2,4},{3,5},{4,6},{5,7},{6,0},{7,1},{8,10},{9,11},{10,... | collective-permute-start | bytes 1572872 | tf_op jit(solution)/shard_map/ppermute | solution.py:29
  133.3 12.0 %collective-permute-start.39 = (bf16[512,512]{1,0:T(8,128)(2,1)S(1)}, bf16[512,512]{1,0:T(8,128)(2,1)S(1)}, u32[]{:S(2)}, u32[]{:S(2)}) collective-permute-start(bf16[512,512]{1,0:T(8,128)(2,1)S(1)} %add_convert_fusion.2), channel_id=1, source_target_pairs={{0,2},{1,3},{2,4},{3,5},{4,6},{5,7},{6,0},{7,1},{8,10},{9,11},{10,... | collective-permute-start | bytes 1572872 | tf_op jit(solution)/shard_map/ppermute | solution.py:29
  138.6 13.7 %collective-permute-start.46 = (bf16[256,1024]{1,0:T(8,128)(2,1)S(1)}, bf16[256,1024]{1,0:T(8,128)(2,1)S(1)}, u32[]{:S(2)}, u32[]{:S(2)}) collective-permute-start(bf16[256,1024]{1,0:T(8,128)(2,1)S(1)} %collective-permute-done.42), channel_id=1, source_target_pairs={{0,9},{1,8},{2,11},{3,10},{4,13},{5,12},{6,15},{7,14},{8,1},{9,0},... | collective-permute-start | bytes 1572872 | tf_op jit(solution)/shard_map/ppermute | solution.py:29
  139.7 10.7 %collective-permute-start.47 = (bf16[256,512]{1,0:T(8,128)(2,1)S(1)}, bf16[256,512]{1,0:T(8,128)(2,1)S(1)}, u32[]{:S(2)}, u32[]{:S(2)}) collective-permute-start(bf16[256,512]{1,0:T(8,128)(2,1)S(1)} %get-tuple-element.134), channel_id=1, source_target_pairs={{0,8},{1,9},{2,10},{3,11},{4,12},{5,13},{6,14},{7,15},{8,0},{9,1},... | collective-permute-start | bytes 786440 | tf_op jit(solution)/shard_map/ppermute | solution.py:29
  154.8 10.7 %collective-permute-start.51 = (bf16[256,1024]{1,0:T(8,128)(2,1)}, bf16[256,1024]{1,0:T(8,128)(2,1)}, u32[]{:S(2)}, u32[]{:S(2)}) collective-permute-start(bf16[256,1024]{1,0:T(8,128)(2,1)} %add_convert_fusion.1), channel_id=1, source_target_pairs={{0,32},{1,33},{2,34},{3,35},{4,36},{5,37},{6,38},{7,39},{8,40},{9,... | collective-permute-start | bytes 1572872 | tf_op jit(solution)/shard_map/ppermute | solution.py:29
  (50 other events, 601.2 us)
